TPU v7x, 32 devices: a whole 2x2x4 slice. The times are simulated.
32 devices in a mesh: dp: 4 (over y, x), expert: 4 (over z), mp: 2 (over core).
Axes of the slice: x: 2, y: 2, z: 4, core: 2. Of those that a mesh axis runs over, the one named last changes fastest.
Arguments:
- tokens: float32 [2048, 1024], P(('dp', 'expert')), may hold values from -6 to 6
- block_experts: int32 [512, 1], P(('dp', 'expert')), may hold values from 0 to 3, as said below
- weight_up: bfloat16 [4, 1024, 2048], P('expert', None, 'mp'), may hold values from -0.1875 to 0.1875
- weight_down: bfloat16 [4, 2048, 1024], P('expert', 'mp'), may hold values from -0.125 to 0.125
- upstream: float32 [2048, 1024], P(('dp', 'expert')), may hold values from -6 to 6
Outputs:
- layer_output: float32 [2048, 1024], P(('dp', 'expert'))
- grad_tokens: float32 [2048, 1024], P(('dp', 'expert'))
- grad_up: float32 [4, 1024, 2048], P('expert', 'dp', 'mp')
- grad_down: float32 [4, 2048, 1024], P('expert', 'mp', 'dp')
Inputs may be any that keep to these rules, and one draw needn't show every extreme that they name: `block_experts`: of the 32 cell blocks of one device, at most 16 name the same expert, and in every draw some expert is named by exactly 16 blocks of every device.
All inputs are finite; a program needn't handle non-finite values.
Results may differ from a plain program's by a relative error of at most 0.015.
Values may be sent and summed in bfloat16 or wider, within the bound.
A program may use at most 64 MiB of HBM per device.

v0:
```python
import jax
import jax.numpy as jnp
from jax import lax
from jax.sharding import PartitionSpec as P


def body(tokens, block_experts, weight_up, weight_down, upstream):
    experts = lax.axis_size("expert")
    blocks_dev = block_experts.shape[0]
    tok_rows = tokens.shape[0]
    width = tokens.shape[1]
    block = tok_rows // blocks_dev
    capacity = max(1, blocks_dev * 2 // experts)
    slot_total = experts * capacity
    labels = block_experts[:, 0]
    order = jnp.arange(blocks_dev, dtype=jnp.int32)
    earlier = order[None, :] < order[:, None]
    matches = labels[:, None] == labels[None, :]
    block_rank = jnp.sum(jnp.logical_and(matches, earlier).astype(jnp.int32), axis=1)
    slot_of_block = labels * capacity + block_rank
    slot_match = slot_of_block[None, :] == jnp.arange(slot_total, dtype=jnp.int32)[:, None]
    source_block = jnp.sum(jnp.where(slot_match, order[None, :], 0), axis=1)
    occupied = jnp.any(slot_match, axis=1)

    def dispatch(rows_lo):
        blocks = rows_lo.reshape(blocks_dev, block, width)
        picked = jnp.take(blocks, source_block, axis=0)
        filled = jnp.where(occupied[:, None, None], picked, jnp.zeros((), rows_lo.dtype))
        outgoing = filled.reshape(experts, capacity * block, width)
        arrived = lax.all_to_all(outgoing, "expert", split_axis=0, concat_axis=0, tiled=True)
        return arrived.reshape(-1, width)

    def bring_home(partial_value):
        shaped = partial_value.reshape(experts, capacity * block, width)
        returned = lax.all_to_all(
            shaped.astype(jnp.bfloat16), "expert", split_axis=0, concat_axis=0, tiled=True
        ).astype(shaped.dtype)
        mine = jnp.take(returned.reshape(slot_total, block, width), slot_of_block, axis=0)
        result = lax.psum(mine.reshape(tok_rows, width).astype(jnp.bfloat16), "mp").astype(
            jnp.float32
        )
        return result

    up_matrix = weight_up[0]
    down_matrix = weight_down[0]
    contract_last = (((1,), (1,)), ((), ()))
    contract_first = (((0,), (0,)), ((), ()))
    routed_lo = dispatch(tokens.astype(jnp.bfloat16))
    pre_act = jnp.dot(routed_lo, up_matrix, preferred_element_type=jnp.float32)
    hidden = jax.nn.gelu(pre_act).astype(jnp.bfloat16)
    mixed_part = jnp.dot(hidden, down_matrix, preferred_element_type=jnp.float32)
    layer_output = tokens + bring_home(mixed_part)
    routed_up = dispatch(upstream.astype(jnp.bfloat16))
    hidden_grad = lax.dot_general(
        routed_up, down_matrix, contract_last, preferred_element_type=jnp.float32
    )
    unused, gelu_back = jax.vjp(jax.nn.gelu, pre_act)
    pre_grad = gelu_back(hidden_grad)[0].astype(jnp.bfloat16)
    token_part = lax.dot_general(
        pre_grad, up_matrix, contract_last, preferred_element_type=jnp.float32
    )
    up_part = lax.dot_general(
        routed_lo, pre_grad, contract_first, preferred_element_type=jnp.float32
    )
    down_part = lax.dot_general(
        hidden, routed_up, contract_first, preferred_element_type=jnp.float32
    )
    grad_tokens = upstream + bring_home(token_part)
    grad_up, grad_down = (
        lax.psum_scatter(
            up_part[None].astype(jnp.bfloat16), "dp", scatter_dimension=1, tiled=True
        ).astype(jnp.float32),
        lax.psum_scatter(
            down_part[None].astype(jnp.bfloat16), "dp", scatter_dimension=2, tiled=True
        ).astype(jnp.float32),
    )
    return (layer_output, grad_tokens, grad_up, grad_down)


def solution(mesh):
    placed = (
        P(("dp", "expert"), None),
        P(("dp", "expert"), None),
        P("expert", None, "mp"),
        P("expert", "mp", None),
        P(("dp", "expert"), None),
    )
    return jax.shard_map(
        body,
        mesh=mesh,
        in_specs=placed,
        out_specs=(
            P(("dp", "expert"), None),
            P(("dp", "expert"), None),
            P("expert", "dp", "mp"),
            P("expert", "mp", "dp"),
        ),
        check_vma=False,
    )
```

profile of v0, /device:TPU:0, one launch (start us, length us, event | category | flops | bytes accessed | tf_op | source)
XLA Modules:
  0.0 183.4 jit_solution(2592968326464980326)
XLA Ops:
  8.0 1.0 convert_reduce_fusion
  9.0 0.7 compare_and_fusion
  9.7 0.1 select_reduce_fusion
  9.8 0.1 fusion.23
  9.9 1.1 convert_element_type.60
  11.0 0.1 reshape.68
  11.1 1.1 convert_element_type.66
  12.2 0.1 reshape.73
  12.3 1.8 gather_fusion
  14.0 1.8 gather_fusion.2
  15.8 1.9 %select_select_fusion = (bf16[64,4,1024]{2,1,0:T(4,128)(2,1)S(1)}, bf16[64,4,1024]{2,1,0:T(4,128)(2,1)S(1)}) fusion(bf16[64,4,1024]{2,1,0:T(4,128)(2,1)} %gather_fusion.2, pred[64]{0:T(512)(128)(4,1)S(1)} %compare_and_fusion.1, pred[64]{0:T(512)(128)(4,1)S(1)} %fusion.23, bf16[64,4,1024]{2,1,0:T(4,128)(2,1)} %gather_fusion), kind=kLoop, calls=%fused_computation.27 | loop fusion | flops 1048576 | bytes 2097280 | tf_op jit(solution)/shard_map/jit(_where)/select_n | solution.py:28
  17.7 0.9 reshape.69
  18.6 6.3 %all-to-all-start = ((bf16[4,64,1024]{2,1,0:T(8,128)(2,1)}), bf16[4,64,1024]{2,1,0:T(8,128)(2,1)S(1)}, u32[]{:S(2)}, u32[]{:S(2)}) async-start(bf16[4,64,1024]{2,1,0:T(8,128)(2,1)} %reshape.69), calls=%async_computation | async-start | bytes 1048576 | tf_op jit(solution)/shard_map/all_to_all | solution.py:30
  24.9 0.9 reshape.74
  25.8 13.6 %all-to-all-done = bf16[4,64,1024]{2,1,0:T(8,128)(2,1)S(1)} async-done(((bf16[4,64,1024]{2,1,0:T(8,128)(2,1)}), bf16[4,64,1024]{2,1,0:T(8,128)(2,1)S(1)}, u32[]{:S(2)}, u32[]{:S(2)}) %all-to-all-start) | async-done | bytes 524320 | tf_op jit(solution)/shard_map/all_to_all | solution.py:30
  39.4 3.5 %all-to-all-start.2 = ((bf16[4,64,1024]{2,1,0:T(8,128)(2,1)}), bf16[4,64,1024]{2,1,0:T(8,128)(2,1)S(1)}, u32[]{:S(2)}, u32[]{:S(2)}) async-start(bf16[4,64,1024]{2,1,0:T(8,128)(2,1)} %reshape.74), calls=%async_computation.2 | async-start | bytes 1048576 | tf_op jit(solution)/shard_map/all_to_all | solution.py:30
  42.9 1.8 multiply_convert_fusion
  44.7 0.8 copy-done.6
  45.5 1.5 fusion.8
  47.1 9.8 %all-to-all-done.2 = bf16[4,64,1024]{2,1,0:T(8,128)(2,1)S(1)} async-done(((bf16[4,64,1024]{2,1,0:T(8,128)(2,1)}), bf16[4,64,1024]{2,1,0:T(8,128)(2,1)S(1)}, u32[]{:S(2)}, u32[]{:S(2)}) %all-to-all-start.2) | async-done | bytes 524320 | tf_op jit(solution)/shard_map/all_to_all | solution.py:30
  56.9 3.5 %all-to-all-start.1 = ((bf16[4,64,1024]{2,1,0:T(8,128)(2,1)}), bf16[4,64,1024]{2,1,0:T(8,128)(2,1)S(1)}, u32[]{:S(2)}, u32[]{:S(2)}) async-start(bf16[4,64,1024]{2,1,0:T(8,128)(2,1)} %fusion.8), calls=%async_computation.1 | async-start | bytes 1048576 | tf_op jit(solution)/shard_map/all_to_all | solution.py:35
  60.3 3.1 %fusion.20 = bf16[256,1024]{1,0:T(8,128)(2,1)S(1)} fusion(f32[256,1024]{1,0:T(8,128)} %get-tuple-element.15, bf16[256,1024]{1,0:T(8,128)(2,1)S(1)} %bitcast.41, bf16[1,1024,1024]{2,1,0:T(8,128)(2,1)} %param.12), kind=kOutput, calls=%fused_computation.24 | convolution fusion | flops 542113792 | bytes 4194304 | tf_op jit(solution)/shard_map/dot_general | solution.py:54
  63.5 0.8 copy-done.7
  64.3 1.5 fusion.11
  65.8 8.5 %all-to-all-done.1 = bf16[4,64,1024]{2,1,0:T(8,128)(2,1)S(1)} async-done(((bf16[4,64,1024]{2,1,0:T(8,128)(2,1)}), bf16[4,64,1024]{2,1,0:T(8,128)(2,1)S(1)}, u32[]{:S(2)}, u32[]{:S(2)}) %all-to-all-start.1) | async-done | bytes 524320 | tf_op jit(solution)/shard_map/all_to_all | solution.py:35
  74.3 3.5 %all-to-all-start.3 = ((bf16[4,64,1024]{2,1,0:T(8,128)(2,1)}), bf16[4,64,1024]{2,1,0:T(8,128)(2,1)S(1)}, u32[]{:S(2)}, u32[]{:S(2)}) async-start(bf16[4,64,1024]{2,1,0:T(8,128)(2,1)} %fusion.11), calls=%async_computation.3 | async-start | bytes 1048576 | tf_op jit(solution)/shard_map/all_to_all | solution.py:35
  77.8 0.0 all-reduce.3.cloned.1.call-start
  77.8 1.0 reshape.79
  78.8 1.8 gather_fusion.1
  80.6 11.1 %all-to-all-done.3 = bf16[4,64,1024]{2,1,0:T(8,128)(2,1)S(1)} async-done(((bf16[4,64,1024]{2,1,0:T(8,128)(2,1)}), bf16[4,64,1024]{2,1,0:T(8,128)(2,1)S(1)}, u32[]{:S(2)}, u32[]{:S(2)}) %all-to-all-start.3) | async-done | bytes 524320 | tf_op jit(solution)/shard_map/all_to_all | solution.py:35
  91.7 1.0 reshape.81
  92.7 1.8 gather_fusion.3
  94.5 1.0 select_convert_fusion
  95.5 1.7 convert_element_type.70
  97.2 0.8 convert_element_type.64
  98.0 0.0 all-reduce.3.cloned.1.call-update
  98.0 0.0 reduce-scatter.5.cloned.1.call-start
  98.1 3.1 %convert_bitcast_fusion = bf16[1,1024,1024]{2,1,0:T(8,128)(2,1)} fusion(bf16[256,1024]{1,0:T(8,128)(2,1)} %copy-done.6, bf16[256,1024]{1,0:T(8,128)(2,1)S(1)} %bitcast.42), kind=kOutput, calls=%fused_computation.12 | convolution fusion | flops 537919488 | bytes 3145728 | tf_op jit(solution)/shard_map/dot_general | solution.py:65
  101.2 0.0 reduce-scatter.5.cloned.1.call-update
  101.2 0.0 reduce-scatter.3.cloned.1.call-start
  101.3 3.3 %convert_bitcast_fusion.1 = bf16[1,1024,1024]{2,1,0:T(8,128)(2,1)} fusion(bf16[256,1024]{1,0:T(8,128)(2,1)} %bitcast.40, bf16[256,1024]{1,0:T(8,128)(2,1)} %copy-done.7), kind=kOutput, calls=%fused_computation.13 | convolution fusion | flops 537919488 | bytes 3145728 | tf_op jit(solution)/shard_map/dot_general | solution.py:62
  104.6 0.0 reduce-scatter.3.cloned.1.call-update
  104.7 11.4 %all-reduce.3.cloned.1.call-done = (bf16[128,1024]{1,0:T(8,128)(2,1)}, bf16[128,1024]{1,0:T(8,128)(2,1)}) async-done(((bf16[128,1024]{1,0:T(8,128)(2,1)}, bf16[128,1024]{1,0:T(8,128)(2,1)}), (bf16[128,1024]{1,0:T(8,128)(2,1)}, bf16[128,1024]{1,0:T(8,128)(2,1)})) %all-reduce.3.cloned.1.call-update) | async-done | bytes 524304 | tf_op jit(solution)/shard_map/psum | solution.py:39
  116.1 2.2 %convert_add_fusion = (f32[128,1024]{1,0:T(8,128)}, f32[128,1024]{1,0:T(8,128)}) fusion(f32[128,1024]{1,0:T(8,128)S(1)} %copy-done.1, bf16[128,1024]{1,0:T(8,128)(2,1)} %get-tuple-element.7, f32[128,1024]{1,0:T(8,128)S(1)} %copy-done.2, bf16[128,1024]{1,0:T(8,128)(2,1)} %get-tuple-element.6), kind=kLoop, calls=%fused_computation.30 | loop fusion | flops 524288 | bytes 2621440 | tf_op jit(solution)/shard_map/add | solution.py:68
  118.2 17.6 %reduce-scatter.5.cloned.1.call-done = bf16[1,1024,256]{2,1,0:T(8,128)(2,1)} async-done(((bf16[1,1024,1024]{2,1,0:T(8,128)(2,1)}), bf16[1,1024,256]{2,1,0:T(8,128)(2,1)}) %reduce-scatter.5.cloned.1.call-update) | async-done | bytes 524304 | tf_op jit(solution)/shard_map/reduce_scatter | solution.py:73
  135.9 2.1 %convert_element_type.77 = f32[1,1024,256]{2,1,0:T(8,128)} convert(bf16[1,1024,256]{2,1,0:T(8,128)(2,1)} %reduce-scatter.5.cloned.1.call-done) | non-fusion elementwise | flops 262144 | bytes 1572864 | tf_op jit(solution)/shard_map/convert_element_type | solution.py:75
  138.0 35.8 %reduce-scatter.3.cloned.1.call-done = bf16[1,256,1024]{2,1,0:T(8,128)(2,1)} async-done(((bf16[1,1024,1024]{2,1,0:T(8,128)(2,1)}), bf16[1,256,1024]{2,1,0:T(8,128)(2,1)}) %reduce-scatter.3.cloned.1.call-update) | async-done | bytes 524304 | tf_op jit(solution)/shard_map/reduce_scatter | solution.py:70
  173.8 2.1 %convert_element_type.74 = f32[1,256,1024]{2,1,0:T(8,128)} convert(bf16[1,256,1024]{2,1,0:T(8,128)(2,1)} %reduce-scatter.3.cloned.1.call-done) | non-fusion elementwise | flops 262144 | bytes 1572864 | tf_op jit(solution)/shard_map/convert_element_type | solution.py:72
  (21 shorter events, 0.1 us)
Async XLA Ops:
  8.0 34.9 %copy-start = (bf16[1,1024,1024]{2,1,0:T(8,128)(2,1)S(1)}, bf16[1,1024,1024]{2,1,0:T(8,128)(2,1)}, u32[]{:S(2)}) copy-start(bf16[1,1024,1024]{2,1,0:T(8,128)(2,1)} %param.11) | copy-start | bytes 6291460
  18.6 20.8 %all-to-all-start = ((bf16[4,64,1024]{2,1,0:T(8,128)(2,1)}), bf16[4,64,1024]{2,1,0:T(8,128)(2,1)S(1)}, u32[]{:S(2)}, u32[]{:S(2)}) async-start(bf16[4,64,1024]{2,1,0:T(8,128)(2,1)} %reshape.69), calls=%async_computation | async-start | bytes 1048576 | tf_op jit(solution)/shard_map/all_to_all | solution.py:30
  39.4 5.3 %copy-start.3 = (bf16[4,64,1024]{2,1,0:T(8,128)(2,1)}, bf16[4,64,1024]{2,1,0:T(8,128)(2,1)S(1)}, u32[]{:S(2)}) copy-start(bf16[4,64,1024]{2,1,0:T(8,128)(2,1)S(1)} %all-to-all-done) | copy-start | bytes 1572868
  39.4 17.4 %all-to-all-start.2 = ((bf16[4,64,1024]{2,1,0:T(8,128)(2,1)}), bf16[4,64,1024]{2,1,0:T(8,128)(2,1)S(1)}, u32[]{:S(2)}, u32[]{:S(2)}) async-start(bf16[4,64,1024]{2,1,0:T(8,128)(2,1)} %reshape.74), calls=%async_computation.2 | async-start | bytes 1048576 | tf_op jit(solution)/shard_map/all_to_all | solution.py:30
  42.9 2.6 %copy-start.8 = (bf16[1,1024,1024]{2,1,0:T(8,128)(2,1)S(1)}, bf16[1,1024,1024]{2,1,0:T(8,128)(2,1)}, u32[]{:S(2)}) copy-start(bf16[1,1024,1024]{2,1,0:T(8,128)(2,1)} %param.12) | copy-start | bytes 6291460
  44.7 0.8 copy-start.6
  56.9 6.6 %copy-start.4 = (bf16[4,64,1024]{2,1,0:T(8,128)(2,1)}, bf16[4,64,1024]{2,1,0:T(8,128)(2,1)S(1)}, u32[]{:S(2)}) copy-start(bf16[4,64,1024]{2,1,0:T(8,128)(2,1)S(1)} %all-to-all-done.2) | copy-start | bytes 1572868
  56.9 17.4 %all-to-all-start.1 = ((bf16[4,64,1024]{2,1,0:T(8,128)(2,1)}), bf16[4,64,1024]{2,1,0:T(8,128)(2,1)S(1)}, u32[]{:S(2)}, u32[]{:S(2)}) async-start(bf16[4,64,1024]{2,1,0:T(8,128)(2,1)} %fusion.8), calls=%async_computation.1 | async-start | bytes 1048576 | tf_op jit(solution)/shard_map/all_to_all | solution.py:35
  63.5 0.8 copy-start.7
  74.3 17.4 %all-to-all-start.3 = ((bf16[4,64,1024]{2,1,0:T(8,128)(2,1)}), bf16[4,64,1024]{2,1,0:T(8,128)(2,1)S(1)}, u32[]{:S(2)}, u32[]{:S(2)}) async-start(bf16[4,64,1024]{2,1,0:T(8,128)(2,1)} %fusion.11), calls=%async_computation.3 | async-start | bytes 1048576 | tf_op jit(solution)/shard_map/all_to_all | solution.py:35
  77.8 38.3 %all-reduce.3.cloned.1.call-start = ((), (), s32[]{:S(2)}) async-start(), calls=%async_computation.8 | async-start | bytes 1048576 | tf_op jit(solution)/shard_map/psum | solution.py:39
  80.6 17.4 %copy-start.5 = (bf16[4,64,1024]{2,1,0:T(8,128)(2,1)S(1)}, bf16[4,64,1024]{2,1,0:T(8,128)(2,1)}, u32[]{:S(2)}) copy-start(bf16[4,64,1024]{2,1,0:T(8,128)(2,1)} %copy-done.4) | copy-start | bytes 1572868
  98.0 37.9 %reduce-scatter.5.cloned.1.call-start = ((), (), s32[]{:S(2)}) async-start(), calls=%async_computation.7 | async-start | bytes 2621440 | tf_op jit(solution)/shard_map/reduce_scatter | solution.py:73
  101.2 14.8 %copy-start.1 = (f32[128,1024]{1,0:T(8,128)S(1)}, f32[128,1024]{1,0:T(8,128)}, u32[]{:S(2)}) copy-start(f32[128,1024]{1,0:T(8,128)} %param.13) | copy-start | bytes 1572868
  101.2 14.8 %copy-start.2 = (f32[128,1024]{1,0:T(8,128)S(1)}, f32[128,1024]{1,0:T(8,128)}, u32[]{:S(2)}) copy-start(f32[128,1024]{1,0:T(8,128)} %param.9) | copy-start | bytes 1572868
  101.2 72.6 %reduce-scatter.3.cloned.1.call-start = ((), (), s32[]{:S(2)}) async-start(), calls=%async_computation.6 | async-start | bytes 2621440 | tf_op jit(solution)/shard_map/reduce_scatter | solution.py:70
Sparse Core Ops, SparseCore 0:
  98.1 17.8 all-reduce.2
Sparse Core Ops, SparseCore 1:
  101.7 34.1 reduce-scatter.4
  138.7 35.0 reduce-scatter.2
where the time goes:
time: 184 us; the launch traced here: 183 us
  waiting for transfers between devices  108 us (59%)
  starting transfers between devices  16.9 us (9%)
  between operations  15.7 us (9%)
  local copies, waits for them, and re-layouts  15.3 us (8%)
  matrix products  14.4 us (8%)
  other arithmetic  13.3 us (7%)
    reduce_scatter x1, waiting for transfers between devices, body(): lax.psum_scatter(up_part[None].astype(jnp.bfloat16), 'dp', scatter_dimens...  35.8 us
    all_to_all x2, waiting for transfers between devices, dispatch(): lax.all_to_all(outgoing, 'expert', split_axis=0, concat_axis=0, tiled=True)  23.4 us
    all_to_all x2, waiting for transfers between devices, bring_home(): lax.all_to_all(shaped.astype(jnp.bfloat16), 'expert', split_axis=0, conca...  19.6 us
    reduce_scatter x1, waiting for transfers between devices, body(): lax.psum_scatter(down_part[None].astype(jnp.bfloat16), 'dp', scatter_dime...  17.6 us
    psum x1, waiting for transfers between devices, bring_home(): lax.psum(mine.reshape(tok_rows, width).astype(jnp.bfloat16), 'mp')  11.4 us
    all_to_all x2, starting transfers between devices, dispatch(): lax.all_to_all(outgoing, 'expert', split_axis=0, concat_axis=0, tiled=True)  9.79 us
    all_to_all x2, starting transfers between devices, bring_home(): lax.all_to_all(shaped.astype(jnp.bfloat16), 'expert', split_axis=0, conca...  6.94 us
    convert_element_type x2, other arithmetic, body(): grad_up, grad_down = (lax.psum_scatter(up_part[None].astype(jnp.bfloat16)...  4.21 us
  transfers between devices with their start and end apart: 7, of which 7 were waited for; matrix products, arithmetic and copies ran while one was open for 12% of the time, Pallas kernels for 0%

commit v1 on v0

--- a/solution.py
+++ b/solution.py
@@ -1,10 +1,420 @@
 import jax
 import jax.numpy as jnp
 from jax import lax
+from jax.experimental import pallas as pl
+from jax.experimental.pallas import tpu as pltpu
 from jax.sharding import PartitionSpec as P
 
-
-def body(tokens, block_experts, weight_up, weight_down, upstream):
+MESH = pl.DeviceIdType.MESH
+LAST = (((1,), (1,)), ((), ()))
+FIRST = (((0,), (0,)), ((), ()))
+F32 = jnp.float32
+BF16 = jnp.bfloat16
+TILE = 256
+
+
+def flip(index, k):
+    if k == 0:
+        return index
+    if k == 1:
+        return index + 1 - 2 * lax.rem(index, 2)
+    if k == 2:
+        return lax.rem(index + 2, 4)
+    return 3 - index
+
+
+def remote(src, dst, send_sem, recv_sem, device):
+    return pltpu.make_async_remote_copy(
+        src_ref=src, dst_ref=dst, send_sem=send_sem, recv_sem=recv_sem, device_id=device, device_id_type=MESH
+    )
+
+
+def finish(first, second, third, fourth, first_out, second_out, third_out, fourth_out, sem):
+    pairs = ((first, first_out), (second, second_out), (third, third_out), (fourth, fourth_out))
+    copies = []
+    for index, (src, dst) in enumerate(pairs):
+        half = src.shape[0] // 2
+        for part in range(2):
+            rows = pl.ds(part * half, half)
+            copies.append(pltpu.make_async_copy(src.at[rows], dst.at[rows], sem.at[2 * index + part]))
+    for copy in copies:
+        copy.start()
+    for copy in copies:
+        copy.wait()
+
+
+def kernel(
+    labels,
+    tokens_hbm,
+    upstream_hbm,
+    up_hbm,
+    down_hbm,
+    layer_out,
+    grad_tokens_out,
+    grad_up_out,
+    grad_down_out,
+    rows_in,
+    up,
+    down,
+    routed,
+    gathered,
+    hidden,
+    slope_kept,
+    pre_grad,
+    parts,
+    parts_in,
+    summed,
+    returned,
+    grad_up,
+    grad_down,
+    load_sem,
+    store_sem,
+    z_send,
+    z_recv,
+    x_send,
+    x_recv,
+    y_send,
+    y_recv,
+    s_send,
+    s_recv,
+    p_send,
+    p_recv,
+    r_send,
+    r_recv,
+    h_send,
+    h_recv,
+):
+    dp = lax.axis_index("dp")
+    me = lax.axis_index("expert")
+    core = lax.axis_index("mp")
+    other = 1 - core
+    tok_rows, width = rows_in.shape[1], rows_in.shape[2]
+    blocks_dev = labels.shape[1]
+    block = tok_rows // blocks_dev
+    slots = routed.shape[1]
+    half = slots // 2
+    piece = half // 4
+    share = grad_up.shape[0]
+    units = up.shape[1]
+
+    loads = [
+        pltpu.make_async_copy(tokens_hbm, rows_in.at[0], load_sem.at[0]),
+        pltpu.make_async_copy(upstream_hbm, rows_in.at[1], load_sem.at[1]),
+        pltpu.make_async_copy(up_hbm, up, load_sem.at[2]),
+        pltpu.make_async_copy(down_hbm, down, load_sem.at[3]),
+    ]
+    for load in loads:
+        load.start()
+
+    x_peer = {"dp": flip(dp, 1)}
+    y_peer = {"dp": flip(dp, 2)}
+    sibling = {"mp": other}
+    z_peers = [{"expert": flip(me, k)} for k in range(4)]
+    barrier = pltpu.get_barrier_semaphore()
+    for peer in z_peers[1:] + [x_peer, y_peer, sibling]:
+        pl.semaphore_signal(barrier, inc=1, device_id=peer, device_id_type=MESH)
+
+    experts_at = lax.broadcasted_iota(jnp.int32, (128, blocks_dev), 0)
+    named = (labels[...] == experts_at).astype(F32)
+    row_at = lax.broadcasted_iota(jnp.int32, (tok_rows, blocks_dev), 0)
+    first_row = lax.broadcasted_iota(jnp.int32, (tok_rows, blocks_dev), 1) * block
+    in_block = jnp.logical_and(row_at >= first_row, row_at < first_row + block)
+    before = row_at >= first_row + block
+    row_expert = lax.dot_general(in_block.astype(F32), named, LAST, preferred_element_type=F32)
+    row_rank = lax.dot_general(before.astype(F32), named, LAST, preferred_element_type=F32)
+    start = lax.broadcasted_iota(jnp.int32, (tok_rows, 128), 1).astype(F32) * piece
+    first_slot = jnp.sum(row_expert * start, axis=1, keepdims=True)
+    place = jnp.sum(row_expert * (block * row_rank), axis=1, keepdims=True)
+    place += jnp.sum(jnp.where(in_block, row_at - first_row, 0).astype(F32), axis=1, keepdims=True)
+    slot_of_row = first_slot + place + jnp.where(place >= piece, float(half - piece), 0.0)
+    slot_at = lax.broadcasted_iota(jnp.int32, (tok_rows, slots), 1).astype(F32)
+    picks = (slot_of_row == slot_at).astype(BF16)
+
+    def one(side, k):
+        return pl.ds(pl.multiple_of(side * half + flip(me, k) * piece, piece), piece)
+
+    def pair(side, p):
+        q = lax.div(me, 2)
+        at = q if p == 0 else 1 - q
+        return pl.ds(pl.multiple_of(side * half + at * (2 * piece), 2 * piece), 2 * piece)
+
+    sent = []
+
+    def go(src, dst, send_sem, recv_sem, peer):
+        copy = remote(src, dst, send_sem, recv_sem, peer)
+        copy.start()
+        sent.append(copy)
+
+    def arrived(dst, send_sem, recv_sem, peer):
+        remote(dst, dst, send_sem, recv_sem, peer).wait_recv()
+
+    def route(a):
+        loads[a].wait()
+        rows_lo = rows_in[a].astype(BF16)
+        routed[a] = lax.dot_general(picks, rows_lo, FIRST, preferred_element_type=F32).astype(BF16)
+
+    def dispatch(a):
+        for k in (2, 3, 1):
+            go(
+                routed.at[a, one(core, k)],
+                gathered.at[a, dp, one(core, 0)],
+                z_send.at[a, k],
+                z_recv.at[a, k],
+                z_peers[k],
+            )
+        gathered[a, dp, one(core, 0), :] = routed[a, one(core, 0), :]
+
+    def block_at(a, rel, p, side=None):
+        return gathered.at[a, flip(dp, rel), pair(core if side is None else side, p)]
+
+    def to_sibling(a, rel, p):
+        go(block_at(a, rel, p), block_at(a, rel, p), s_send.at[a, rel, p], s_recv.at[a, rel, p], sibling)
+
+    def from_sibling(a, rel):
+        for p in range(2):
+            arrived(block_at(a, rel, p, other), s_send.at[a, rel, p], s_recv.at[a, rel, p], sibling)
+
+    def spread(a, p):
+        for k in (2 * p, 2 * p + 1):
+            if k:
+                arrived(gathered.at[a, dp, one(core, k)], z_send.at[a, k], z_recv.at[a, k], z_peers[k])
+        to_sibling(a, 0, p)
+        go(block_at(a, 0, p), block_at(a, 0, p), x_send.at[a, p], x_recv.at[a, p], x_peer)
+        go(block_at(a, 0, p), block_at(a, 0, p), y_send.at[a, p], y_recv.at[a, p], y_peer)
+
+    def pass_on(a, p):
+        arrived(block_at(a, 1, p), x_send.at[a, p], x_recv.at[a, p], x_peer)
+        if p == 0:
+            go(block_at(a, 1, 0), block_at(a, 1, 0), y_send.at[a, 2], y_recv.at[a, 2], y_peer)
+        to_sibling(a, 1, p)
+        arrived(block_at(a, 2, p), y_send.at[a, p], y_recv.at[a, p], y_peer)
+        if p == 1:
+            go(block_at(a, 2, 1), block_at(a, 2, 1), x_send.at[a, 2], x_recv.at[a, 2], x_peer)
+        to_sibling(a, 2, p)
+
+    def from_corner(a):
+        arrived(block_at(a, 3, 0), y_send.at[a, 2], y_recv.at[a, 2], y_peer)
+        to_sibling(a, 3, 0)
+        arrived(block_at(a, 3, 1), x_send.at[a, 2], x_recv.at[a, 2], x_peer)
+        to_sibling(a, 3, 1)
+
+    mine_cols = pl.ds(pl.multiple_of(dp * share, share), share)
+
+    def activation(value):
+        scale = 0.7978845608028654
+        square = value * value
+        turn = jnp.tanh(value * (scale + (scale * 0.044715) * square))
+        cdf = 0.5 + 0.5 * turn
+        slope = cdf + value * (0.5 - 0.5 * turn * turn) * (scale + (3 * scale * 0.044715) * square)
+        return (value * cdf).astype(BF16), slope
+
+    def tiles(total, step):
+        def run(index, carry):
+            step(pl.ds(pl.multiple_of(index * TILE, TILE), TILE))
+            return carry
+
+        lax.fori_loop(0, total // TILE, run, 0)
+
+    def forward(cols):
+        value = jnp.dot(gathered[0, dp], up[:, cols], preferred_element_type=F32)
+        hidden[:, cols], slope_kept[:, cols] = activation(value)
+
+    def mix(cols):
+        parts[0, :, cols] = jnp.dot(hidden[...], down[:, cols], preferred_element_type=F32).astype(BF16)
+
+    def backward(cols):
+        back = lax.dot_general(gathered[1, dp], down[cols, :], LAST, preferred_element_type=F32)
+        pre_grad[:, cols] = (back * slope_kept[:, cols]).astype(BF16)
+
+    def unmix(cols):
+        parts[1, :, cols] = lax.dot_general(
+            pre_grad[...], up[cols, :], LAST, preferred_element_type=F32
+        ).astype(BF16)
+
+    def own_grads(cols):
+        grad_up[:, cols] = lax.dot_general(
+            gathered[0, dp, :, mine_cols], pre_grad[:, cols], FIRST, preferred_element_type=F32
+        )
+        grad_down[cols, :] = lax.dot_general(
+            hidden[:, cols], gathered[1, dp, :, mine_cols], FIRST, preferred_element_type=F32
+        )
+
+    def other_grads(rel):
+        at = flip(dp, rel)
+
+        def step(cols):
+            value = jnp.dot(gathered[0, at], up[:, cols], preferred_element_type=F32)
+            back = lax.dot_general(gathered[1, at], down[cols, :], LAST, preferred_element_type=F32)
+            hidden_lo, slope = activation(value)
+            grad_lo = (back * slope).astype(BF16)
+            grad_up[:, cols] += lax.dot_general(
+                gathered[0, at, :, mine_cols], grad_lo, FIRST, preferred_element_type=F32
+            )
+            grad_down[cols, :] += lax.dot_general(
+                hidden_lo, gathered[1, at, :, mine_cols], FIRST, preferred_element_type=F32
+            )
+
+        tiles(units, step)
+
+    def swap(a):
+        theirs = pl.ds(pl.multiple_of(other * half, half), half)
+        go(parts.at[a, theirs], parts_in.at[a], p_send.at[a], p_recv.at[a], sibling)
+
+    def send_home(a):
+        arrived(parts_in.at[a], p_send.at[a], p_recv.at[a], sibling)
+        ours = pl.ds(pl.multiple_of(core * half, half), half)
+        summed[a] = (parts[a, ours, :].astype(F32) + parts_in[a].astype(F32)).astype(BF16)
+        for k in (2, 3, 1):
+            go(
+                summed.at[a, pl.ds(pl.multiple_of(flip(me, k) * piece, piece), piece)],
+                returned.at[a, one(core, 0)],
+                r_send.at[a, k],
+                r_recv.at[a, k],
+                z_peers[k],
+            )
+        returned[a, one(core, 0), :] = summed[a, pl.ds(pl.multiple_of(me * piece, piece), piece), :]
+
+    def reach_home(a, p):
+        for k in (2 * p, 2 * p + 1):
+            if k:
+                arrived(returned.at[a, one(core, k)], r_send.at[a, k], r_recv.at[a, k], z_peers[k])
+        block = returned.at[a, pair(core, p)]
+        go(block, block, h_send.at[a, p], h_recv.at[a, p], sibling)
+
+    stores = []
+
+    def store(src, dst):
+        copy = pltpu.make_async_copy(src, dst, store_sem.at[len(stores)])
+        copy.start()
+        stores.append(copy)
+
+    def add_home(a, out):
+        for p in range(2):
+            arrived(returned.at[a, pair(other, p)], h_send.at[a, p], h_recv.at[a, p], sibling)
+        rows_in[a] += jnp.dot(picks, returned[a], preferred_element_type=F32)
+        store(rows_in.at[a], out)
+
+    route(0)
+    pl.semaphore_wait(barrier, 6)
+    dispatch(0)
+    route(1)
+    spread(0, 0)
+    dispatch(1)
+    pass_on(0, 0)
+    spread(0, 1)
+    loads[2].wait()
+    loads[3].wait()
+    from_sibling(0, 0)
+    tiles(units, forward)
+    tiles(width, mix)
+    swap(0)
+    spread(1, 0)
+    pass_on(0, 1)
+    send_home(0)
+    pass_on(1, 0)
+    spread(1, 1)
+    from_sibling(1, 0)
+    tiles(units, backward)
+    tiles(width, unmix)
+    swap(1)
+    from_corner(0)
+    pass_on(1, 1)
+    send_home(1)
+    tiles(units, own_grads)
+    for a in range(2):
+        from_sibling(a, 1)
+    other_grads(1)
+    from_corner(1)
+    for a in range(2):
+        from_sibling(a, 2)
+    other_grads(2)
+    reach_home(0, 0)
+    reach_home(0, 1)
+    for a in range(2):
+        from_sibling(a, 3)
+    other_grads(3)
+    store(grad_up, grad_up_out)
+    store(grad_down, grad_down_out)
+    reach_home(1, 0)
+    add_home(0, layer_out)
+    reach_home(1, 1)
+    add_home(1, grad_tokens_out)
+    for copy in sent:
+        copy.wait_send()
+    for copy in stores:
+        copy.wait()
+
+
+def fused_body(tokens, block_experts, weight_up, weight_down, upstream):
+    tok_rows, width = tokens.shape
+    blocks_dev = block_experts.shape[0]
+    units = weight_up.shape[2]
+    slots = 2 * tok_rows
+    half = slots // 2
+    share = width // 4
+    in_hbm = pl.BlockSpec(memory_space=pltpu.HBM)
+    anywhere = pl.BlockSpec(memory_space=pl.ANY)
+    flops = 2 * slots * width * units * 12
+    results = (
+        jax.ShapeDtypeStruct((tok_rows, width), F32),
+        jax.ShapeDtypeStruct((tok_rows, width), F32),
+        jax.ShapeDtypeStruct((share, units), F32),
+        jax.ShapeDtypeStruct((units, share), F32),
+    )
+    held = pl.pallas_call(
+        kernel,
+        out_shape=results,
+        in_specs=[pl.BlockSpec(memory_space=pltpu.VMEM)] + [in_hbm] * 4,
+        out_specs=(anywhere,) * 4,
+        scratch_shapes=[
+            pltpu.VMEM((2, tok_rows, width), F32),
+            pltpu.VMEM((width, units), BF16),
+            pltpu.VMEM((units, width), BF16),
+            pltpu.VMEM((2, slots, width), BF16),
+            pltpu.VMEM((2, 4, slots, width), BF16),
+            pltpu.VMEM((slots, units), BF16),
+            pltpu.VMEM((slots, units), F32),
+            pltpu.VMEM((slots, units), BF16),
+            pltpu.VMEM((2, slots, width), BF16),
+            pltpu.VMEM((2, half, width), BF16),
+            pltpu.VMEM((2, half, width), BF16),
+            pltpu.VMEM((2, slots, width), BF16),
+            pltpu.VMEM((share, units), F32),
+            pltpu.VMEM((units, share), F32),
+            pltpu.SemaphoreType.DMA((4,)),
+            pltpu.SemaphoreType.DMA((4,)),
+            pltpu.SemaphoreType.DMA((2, 4)),
+            pltpu.SemaphoreType.DMA((2, 4)),
+            pltpu.SemaphoreType.DMA((2, 3)),
+            pltpu.SemaphoreType.DMA((2, 3)),
+            pltpu.SemaphoreType.DMA((2, 3)),
+            pltpu.SemaphoreType.DMA((2, 3)),
+            pltpu.SemaphoreType.DMA((2, 4, 2)),
+            pltpu.SemaphoreType.DMA((2, 4, 2)),
+            pltpu.SemaphoreType.DMA((2,)),
+            pltpu.SemaphoreType.DMA((2,)),
+            pltpu.SemaphoreType.DMA((2, 4)),
+            pltpu.SemaphoreType.DMA((2, 4)),
+            pltpu.SemaphoreType.DMA((2, 2)),
+            pltpu.SemaphoreType.DMA((2, 2)),
+        ],
+        compiler_params=pltpu.CompilerParams(
+            collective_id=0, has_side_effects=True, vmem_limit_bytes=40 * 1024 * 1024
+        ),
+        cost_estimate=pl.CostEstimate(flops=flops, bytes_accessed=8 << 20, transcendentals=slots * units * 4),
+    )(block_experts.reshape(1, blocks_dev), tokens, upstream, weight_up[0], weight_down[0])
+    layer_output, grad_tokens, grad_up, grad_down = pl.pallas_call(
+        finish,
+        out_shape=results,
+        in_specs=[anywhere] * 4,
+        out_specs=(in_hbm,) * 4,
+        scratch_shapes=[pltpu.SemaphoreType.DMA((8,))],
+        cost_estimate=pl.CostEstimate(flops=0, bytes_accessed=3 << 20, transcendentals=0),
+    )(*held)
+    return layer_output, grad_tokens, grad_up[None], grad_down[None]
+
+
+def plain_body(tokens, block_experts, weight_up, weight_down, upstream):
     experts = lax.axis_size("expert")
     blocks_dev = block_experts.shape[0]
     tok_rows = tokens.shape[0]
@@ -85,6 +495,20 @@
         P("expert", "mp", None),
         P(("dp", "expert"), None),
     )
+
+    def body(tokens, block_experts, weight_up, weight_down, upstream):
+        tok_rows, width = tokens.shape
+        blocks_dev = block_experts.shape[0]
+        fits = (
+            (mesh.shape["dp"], mesh.shape["expert"], mesh.shape["mp"]) == (4, 4, 2)
+            and blocks_dev % 2 == 0
+            and (tok_rows // 4) % 16 == 0
+            and width % (4 * TILE) == 0
+            and weight_up.shape[2] % TILE == 0
+        )
+        chosen = fused_body if fits else plain_body
+        return chosen(tokens, block_experts, weight_up, weight_down, upstream)
+
     return jax.shard_map(
         body,
         mesh=mesh,

time: 184 us -> 151 us (0.82)
  Pallas kernels: 0 us -> 140 us
  waiting for transfers between devices: 108 us -> 0 us
  starting transfers between devices: 16.9 us -> 0 us
  between operations: 15.7 us -> 0.66 us
  matrix products: 14.4 us -> 0 us
  other arithmetic: 13.3 us -> 0 us
  local copies, waits for them, and re-layouts: 15.3 us -> 9.5 us
    pallas_call x0 -> x2, Pallas kernels: none -> 140 us  [the longest x1 96.5 us: fused_body(): pl.pallas_call(finish, out_shape=results, in_specs=[anywhere] * 4, out_sp...]
    reduce_scatter x2 -> x0, waiting for transfers between devices: 53.5 us -> none  [the longest x1 35.8 us: body(): lax.psum_scatter(up_part[None].astype(jnp.bfloat16), 'dp', scatter_dimens...]
    all_to_all x4 -> x0, waiting for transfers between devices: 42.9 us -> none  [the longest x2 23.4 us: dispatch(): lax.all_to_all(outgoing, 'expert', split_axis=0, concat_axis=0, tiled=True)]
    all_to_all x4 -> x0, starting transfers between devices: 16.7 us -> none  [the longest x2 9.79 us: dispatch(): lax.all_to_all(outgoing, 'expert', split_axis=0, concat_axis=0, tiled=True)]
    dot_general x6 -> x0, matrix products: 14.4 us -> none  [the longest x1 3.34 us: body(): lax.dot_general(routed_lo, pre_grad, contract_first, preferred_element_ty...]
    psum x1 -> x0, waiting for transfers between devices: 11.4 us -> none  [bring_home(): lax.psum(mine.reshape(tok_rows, width).astype(jnp.bfloat16), 'mp')]
    unnamed x18, local copies, waits for them, and re-layouts: 1.63 us -> 9.5 us
    convert_element_type x5 -> x0, other arithmetic: 7.35 us -> none  [the longest x2 4.21 us: body(): grad_up, grad_down = (lax.psum_scatter(up_part[None].astype(jnp.bfloat16)...]
  transfers between devices with their start and end apart: 7 -> 0, of which waited for: 7 -> 0; matrix products, arithmetic and copies ran while one was open for 12% -> 0% of each run, Pallas kernels for 0% -> 0%
where the time goes in v1:
time: 151 us; the launch traced here: 150 us
  Pallas kernels  140 us (93%)
  local copies, waits for them, and re-layouts  9.5 us (6%)
    pallas_call x1, Pallas kernels, fused_body(): pl.pallas_call(finish, out_shape=results, in_specs=[anywhere] * 4, out_sp...  96.5 us
    pallas_call x1, Pallas kernels, fused_body(): pl.pallas_call(kernel, out_shape=results, in_specs=[pl.BlockSpec(memory_s...  43.5 us
    unnamed x18, local copies, waits for them, and re-layouts  9.5 us

profile of v1, /device:TPU:0, one launch (start us, length us, event | category | flops | bytes accessed | tf_op | source)
XLA Modules:
  0.0 150.1 jit_solution(4230120836157212550)
XLA Ops:
  0.6 0.0 copy-start.4
  0.6 1.6 %copy-done.4 = bf16[1,1024,1024]{2,1,0:T(8,128)(2,1)S(1)} copy-done((bf16[1,1024,1024]{2,1,0:T(8,128)(2,1)S(1)}, bf16[1,1024,1024]{2,1,0:T(8,128)(2,1)}, u32[]{:S(2)}) %copy-start.4) | copy-done | bytes 2097176
  2.2 0.0 copy-start.5
  2.2 1.6 %copy-done.5 = bf16[1,1024,1024]{2,1,0:T(8,128)(2,1)S(1)} copy-done((bf16[1,1024,1024]{2,1,0:T(8,128)(2,1)S(1)}, bf16[1,1024,1024]{2,1,0:T(8,128)(2,1)}, u32[]{:S(2)}) %copy-start.5) | copy-done | bytes 2097176
  3.8 0.0 copy-start.6
  3.8 1.0 copy-done.6
  4.9 0.0 copy-start.7
  4.9 1.0 copy-done.7
  5.9 0.0 copy-start.8
  5.9 0.7 copy-done.8
  6.6 43.5 %shard_map.84 = (f32[128,1024]{1,0:T(8,128)S(1)}, f32[128,1024]{1,0:T(8,128)S(1)}, f32[256,1024]{1,0:T(8,128)S(1)}, f32[1024,256]{1,0:T(8,128)S(1)}) custom-call(s32[1,32]{1,0:T(1,128)S(1)} %bitcast.7, f32[128,1024]{1,0:T(8,128)S(1)} %copy-done.6, f32[128,1024]{1,0:T(8,128)S(1)} %copy-done.7, bf16[1024,1024]{1,0:T(8,128)(2,1)S(1)} %bitcast.5, ...), custom_call_target="tpu_custom_call" | custom-call | flops 6442450944 | bytes 8388608 | tf_op jit(solution)/shard_map/pallas_call | solution.py:364
  50.0 0.0 copy-start
  50.1 1.0 copy-done
  51.0 0.0 copy-start.1
  51.0 1.0 copy-done.1
  52.0 0.0 copy-start.2
  52.0 0.8 copy-done.2
  52.9 0.0 copy-start.3
  52.9 0.8 copy-done.3
  53.6 96.5 %shard_map.85 = (f32[128,1024]{1,0:T(8,128)}, f32[128,1024]{1,0:T(8,128)}, f32[256,1024]{1,0:T(8,128)}, f32[1024,256]{1,0:T(8,128)}) custom-call(f32[128,1024]{1,0:T(8,128)} %copy-done.2, f32[128,1024]{1,0:T(8,128)} %copy-done.3, f32[256,1024]{1,0:T(8,128)} %copy-done, f32[1024,256]{1,0:T(8,128)} %copy-done.1), custom_call_target="tpu_custom_call" | custom-call | bytes 3145728 | tf_op jit(solution)/shard_map/pallas_call | solution.py:406
Async XLA Ops:
  0.6 1.6 %copy-start.4 = (bf16[1,1024,1024]{2,1,0:T(8,128)(2,1)S(1)}, bf16[1,1024,1024]{2,1,0:T(8,128)(2,1)}, u32[]{:S(2)}) copy-start(bf16[1,1024,1024]{2,1,0:T(8,128)(2,1)} %param.7) | copy-start | bytes 6291460
  2.2 1.6 %copy-start.5 = (bf16[1,1024,1024]{2,1,0:T(8,128)(2,1)S(1)}, bf16[1,1024,1024]{2,1,0:T(8,128)(2,1)}, u32[]{:S(2)}) copy-start(bf16[1,1024,1024]{2,1,0:T(8,128)(2,1)} %param.8) | copy-start | bytes 6291460
  3.8 1.0 copy-start.6
  4.9 1.0 copy-start.7
  5.9 0.7 copy-start.8
  50.0 1.0 copy-start
  51.0 1.0 copy-start.1
  52.0 0.8 copy-start.2
  52.9 0.8 copy-start.3

commit v2 on v1

--- a/solution.py
+++ b/solution.py
@@ -11,6 +11,7 @@
 F32 = jnp.float32
 BF16 = jnp.bfloat16
 TILE = 256
+GRANT = 57 * 1024 * 1024
 
 
 def flip(index, k):
@@ -29,18 +30,24 @@
     )
 
 
-def finish(first, second, third, fourth, first_out, second_out, third_out, fourth_out, sem):
-    pairs = ((first, first_out), (second, second_out), (third, third_out), (fourth, fourth_out))
-    copies = []
-    for index, (src, dst) in enumerate(pairs):
+def finish(*refs):
+    sources, results, held = refs[:4], refs[4:8], refs[8:12]
+    in_sem, out_sem = refs[12:]
+    loads, stores = [], []
+    for src, dst, kept in zip(sources, results, held):
         half = src.shape[0] // 2
         for part in range(2):
             rows = pl.ds(part * half, half)
-            copies.append(pltpu.make_async_copy(src.at[rows], dst.at[rows], sem.at[2 * index + part]))
-    for copy in copies:
-        copy.start()
-    for copy in copies:
-        copy.wait()
+            index = len(loads)
+            loads.append(pltpu.make_async_copy(src.at[rows], kept.at[rows], in_sem.at[index]))
+            stores.append(pltpu.make_async_copy(kept.at[rows], dst.at[rows], out_sem.at[index]))
+    for load in loads:
+        load.start()
+    for load, store in zip(loads, stores):
+        load.wait()
+        store.start()
+    for store in stores:
+        store.wait()
 
 
 def kernel(
@@ -209,11 +216,8 @@
         return (value * cdf).astype(BF16), slope
 
     def tiles(total, step):
-        def run(index, carry):
-            step(pl.ds(pl.multiple_of(index * TILE, TILE), TILE))
-            return carry
-
-        lax.fori_loop(0, total // TILE, run, 0)
+        for index in range(total // TILE):
+            step(pl.ds(index * TILE, TILE))
 
     def forward(cols):
         value = jnp.dot(gathered[0, dp], up[:, cols], preferred_element_type=F32)
@@ -309,18 +313,18 @@
     tiles(width, mix)
     swap(0)
     spread(1, 0)
+    spread(1, 1)
+    send_home(0)
     pass_on(0, 1)
-    send_home(0)
-    pass_on(1, 0)
-    spread(1, 1)
     from_sibling(1, 0)
     tiles(units, backward)
     tiles(width, unmix)
     swap(1)
+    pass_on(1, 0)
+    tiles(units, own_grads)
+    send_home(1)
     from_corner(0)
     pass_on(1, 1)
-    send_home(1)
-    tiles(units, own_grads)
     for a in range(2):
         from_sibling(a, 1)
     other_grads(1)
@@ -399,7 +403,7 @@
             pltpu.SemaphoreType.DMA((2, 2)),
         ],
         compiler_params=pltpu.CompilerParams(
-            collective_id=0, has_side_effects=True, vmem_limit_bytes=40 * 1024 * 1024
+            collective_id=0, has_side_effects=True, vmem_limit_bytes=GRANT
         ),
         cost_estimate=pl.CostEstimate(flops=flops, bytes_accessed=8 << 20, transcendentals=slots * units * 4),
     )(block_experts.reshape(1, blocks_dev), tokens, upstream, weight_up[0], weight_down[0])
@@ -408,7 +412,9 @@
         out_shape=results,
         in_specs=[anywhere] * 4,
         out_specs=(in_hbm,) * 4,
-        scratch_shapes=[pltpu.SemaphoreType.DMA((8,))],
+        scratch_shapes=[pltpu.VMEM(result.shape, F32) for result in results]
+        + [pltpu.SemaphoreType.DMA((8,)), pltpu.SemaphoreType.DMA((8,))],
+        compiler_params=pltpu.CompilerParams(vmem_limit_bytes=GRANT),
         cost_estimate=pl.CostEstimate(flops=0, bytes_accessed=3 << 20, transcendentals=0),
     )(*held)
     return layer_output, grad_tokens, grad_up[None], grad_down[None]

time: 151 us -> 45.4 us (0.30)
  the two profiles are of different devices: /device:TPU:0 before, /device:TPU:11 now
where the time goes in v2:
time: 45.4 us; the launch traced here: 45.3 us
  Pallas kernels  44.6 us (98%)
  between operations  0.64 us (1%)
    pallas_call x1, Pallas kernels, fused_body(): pl.pallas_call(kernel, out_shape=results, in_specs=[pl.BlockSpec(memory_s...  41.8 us
    pallas_call x1, Pallas kernels, fused_body(): pl.pallas_call(finish, out_shape=results, in_specs=[anywhere] * 4, out_sp...  2.81 us

profile of v2, /device:TPU:11, one launch (start us, length us, event | category | flops | bytes accessed | tf_op | source)
XLA Modules:
  0.0 45.3 jit_solution(2247111858326858456)
XLA Ops:
  0.6 41.8 %shard_map.84 = (f32[128,1024]{1,0:T(8,128)}, f32[128,1024]{1,0:T(8,128)}, f32[256,1024]{1,0:T(8,128)}, f32[1024,256]{1,0:T(8,128)}) custom-call(s32[1,32]{1,0:T(1,128)} %bitcast.9, f32[128,1024]{1,0:T(8,128)} %tokens_hbm.1, f32[128,1024]{1,0:T(8,128)} %upstream_hbm.1, bf16[1024,1024]{1,0:T(8,128)(2,1)} %bitcast.5, bf16[1024,1024]{1,0:T(8,128)(2,1)} %bitcast.6), custom_call_target="tpu_custom_call" | custom-call | flops 6442450944 | bytes 8388608 | tf_op jit(solution)/shard_map/pallas_call | solution.py:368
  42.5 2.8 %shard_map.85 = (f32[128,1024]{1,0:T(8,128)}, f32[128,1024]{1,0:T(8,128)}, f32[256,1024]{1,0:T(8,128)}, f32[1024,256]{1,0:T(8,128)}) custom-call(f32[128,1024]{1,0:T(8,128)} %get-tuple-element.12.refs_0_, f32[128,1024]{1,0:T(8,128)} %get-tuple-element.13.refs_1_, f32[256,1024]{1,0:T(8,128)} %get-tuple-element.14.refs_2_, f32[1024,256]{1,0:T(8,128)} %get-tuple-element.15.refs_3_), custom_call_target="tpu_custom_call" | custom-call | bytes 3145728 | tf_op jit(solution)/shard_map/pallas_call | solution.py:410

commit v3 on v2

--- a/solution.py
+++ b/solution.py
@@ -74,6 +74,8 @@
     returned,
     grad_up,
     grad_down,
+    grad_down_turned,
+    shares,
     load_sem,
     store_sem,
     z_send,
@@ -161,7 +163,7 @@
         routed[a] = lax.dot_general(picks, rows_lo, FIRST, preferred_element_type=F32).astype(BF16)
 
     def dispatch(a):
-        for k in (2, 3, 1):
+        for k in (1, 2, 3):
             go(
                 routed.at[a, one(core, k)],
                 gathered.at[a, dp, one(core, 0)],
@@ -235,30 +237,30 @@
             pre_grad[...], up[cols, :], LAST, preferred_element_type=F32
         ).astype(BF16)
 
+    def turn_shares(rel):
+        for a in range(2):
+            shares[a] = gathered[a, flip(dp, rel), :, mine_cols].T
+
     def own_grads(cols):
-        grad_up[:, cols] = lax.dot_general(
-            gathered[0, dp, :, mine_cols], pre_grad[:, cols], FIRST, preferred_element_type=F32
-        )
-        grad_down[cols, :] = lax.dot_general(
-            hidden[:, cols], gathered[1, dp, :, mine_cols], FIRST, preferred_element_type=F32
-        )
+        grad_up[:, cols] = jnp.dot(shares[0], pre_grad[:, cols], preferred_element_type=F32)
+        grad_down_turned[:, cols] = jnp.dot(shares[1], hidden[:, cols], preferred_element_type=F32)
 
     def other_grads(rel):
         at = flip(dp, rel)
+        turn_shares(rel)
 
         def step(cols):
             value = jnp.dot(gathered[0, at], up[:, cols], preferred_element_type=F32)
             back = lax.dot_general(gathered[1, at], down[cols, :], LAST, preferred_element_type=F32)
             hidden_lo, slope = activation(value)
             grad_lo = (back * slope).astype(BF16)
-            grad_up[:, cols] += lax.dot_general(
-                gathered[0, at, :, mine_cols], grad_lo, FIRST, preferred_element_type=F32
-            )
-            grad_down[cols, :] += lax.dot_general(
-                hidden_lo, gathered[1, at, :, mine_cols], FIRST, preferred_element_type=F32
-            )
+            grad_up[:, cols] += jnp.dot(shares[0], grad_lo, preferred_element_type=F32)
+            grad_down_turned[:, cols] += jnp.dot(shares[1], hidden_lo, preferred_element_type=F32)
 
         tiles(units, step)
+
+    def turn_down(cols):
+        grad_down[cols, :] = grad_down_turned[:, cols].T
 
     def swap(a):
         theirs = pl.ds(pl.multiple_of(other * half, half), half)
@@ -306,28 +308,29 @@
     dispatch(1)
     pass_on(0, 0)
     spread(0, 1)
+    spread(1, 0)
     loads[2].wait()
     loads[3].wait()
     from_sibling(0, 0)
     tiles(units, forward)
     tiles(width, mix)
     swap(0)
-    spread(1, 0)
+    pass_on(0, 1)
+    send_home(0)
+    pass_on(1, 0)
     spread(1, 1)
-    send_home(0)
-    pass_on(0, 1)
     from_sibling(1, 0)
     tiles(units, backward)
     tiles(width, unmix)
     swap(1)
-    pass_on(1, 0)
+    pass_on(1, 1)
+    turn_shares(0)
     tiles(units, own_grads)
     send_home(1)
-    from_corner(0)
-    pass_on(1, 1)
     for a in range(2):
         from_sibling(a, 1)
     other_grads(1)
+    from_corner(0)
     from_corner(1)
     for a in range(2):
         from_sibling(a, 2)
@@ -338,6 +341,7 @@
         from_sibling(a, 3)
     other_grads(3)
     store(grad_up, grad_up_out)
+    tiles(units, turn_down)
     store(grad_down, grad_down_out)
     reach_home(1, 0)
     add_home(0, layer_out)
@@ -385,6 +389,8 @@
             pltpu.VMEM((2, slots, width), BF16),
             pltpu.VMEM((share, units), F32),
             pltpu.VMEM((units, share), F32),
+            pltpu.VMEM((share, units), F32),
+            pltpu.VMEM((2, share, slots), BF16),
             pltpu.SemaphoreType.DMA((4,)),
             pltpu.SemaphoreType.DMA((4,)),
             pltpu.SemaphoreType.DMA((2, 4)),

time: 45.4 us -> 45 us (level)
  the two profiles are of different devices: /device:TPU:11 before, /device:TPU:0 now
where the time goes in v3:
time: 45 us; the launch traced here: 44.2 us
  Pallas kernels  43.6 us (97%)
  between operations  0.64 us (1%)
    pallas_call x1, Pallas kernels, fused_body(): pl.pallas_call(kernel, out_shape=results, in_specs=[pl.BlockSpec(memory_s...  40.8 us
    pallas_call x1, Pallas kernels, fused_body(): pl.pallas_call(finish, out_shape=results, in_specs=[anywhere] * 4, out_sp...  2.81 us

profile of v3, /device:TPU:0, one launch (start us, length us, event | category | flops | bytes accessed | tf_op | source)
XLA Modules:
  0.0 44.2 jit_solution(3489632632827532474)
XLA Ops:
  0.6 40.8 %shard_map.84 = (f32[128,1024]{1,0:T(8,128)}, f32[128,1024]{1,0:T(8,128)}, f32[256,1024]{1,0:T(8,128)}, f32[1024,256]{1,0:T(8,128)}) custom-call(s32[1,32]{1,0:T(1,128)} %bitcast.9, f32[128,1024]{1,0:T(8,128)} %tokens_hbm.1, f32[128,1024]{1,0:T(8,128)} %upstream_hbm.1, bf16[1024,1024]{1,0:T(8,128)(2,1)} %bitcast.5, bf16[1024,1024]{1,0:T(8,128)(2,1)} %bitcast.6), custom_call_target="tpu_custom_call" | custom-call | flops 6442450944 | bytes 8388608 | tf_op jit(solution)/shard_map/pallas_call | solution.py:372
  41.4 2.8 %shard_map.85 = (f32[128,1024]{1,0:T(8,128)}, f32[128,1024]{1,0:T(8,128)}, f32[256,1024]{1,0:T(8,128)}, f32[1024,256]{1,0:T(8,128)}) custom-call(f32[128,1024]{1,0:T(8,128)} %get-tuple-element.12.refs_0_, f32[128,1024]{1,0:T(8,128)} %get-tuple-element.13.refs_1_, f32[256,1024]{1,0:T(8,128)} %get-tuple-element.14.refs_2_, f32[1024,256]{1,0:T(8,128)} %get-tuple-element.15.refs_3_), custom_call_target="tpu_custom_call" | custom-call | bytes 3145728 | tf_op jit(solution)/shard_map/pallas_call | solution.py:416

commit v4 on v3

--- a/solution.py
+++ b/solution.py
@@ -162,15 +162,16 @@
         rows_lo = rows_in[a].astype(BF16)
         routed[a] = lax.dot_general(picks, rows_lo, FIRST, preferred_element_type=F32).astype(BF16)
 
-    def dispatch(a):
-        for k in (1, 2, 3):
-            go(
-                routed.at[a, one(core, k)],
-                gathered.at[a, dp, one(core, 0)],
-                z_send.at[a, k],
-                z_recv.at[a, k],
-                z_peers[k],
-            )
+    def dispatch(a, k):
+        go(
+            routed.at[a, one(core, k)],
+            gathered.at[a, dp, one(core, 0)],
+            z_send.at[a, k],
+            z_recv.at[a, k],
+            z_peers[k],
+        )
+
+    def keep_own(a):
         gathered[a, dp, one(core, 0), :] = routed[a, one(core, 0), :]
 
     def block_at(a, rel, p, side=None):
@@ -187,6 +188,8 @@
         for k in (2 * p, 2 * p + 1):
             if k:
                 arrived(gathered.at[a, dp, one(core, k)], z_send.at[a, k], z_recv.at[a, k], z_peers[k])
+                if a == 0:
+                    dispatch(1, k)
         to_sibling(a, 0, p)
         go(block_at(a, 0, p), block_at(a, 0, p), x_send.at[a, p], x_recv.at[a, p], x_peer)
         go(block_at(a, 0, p), block_at(a, 0, p), y_send.at[a, p], y_recv.at[a, p], y_peer)
@@ -302,10 +305,12 @@
 
     route(0)
     pl.semaphore_wait(barrier, 6)
-    dispatch(0)
+    for k in (1, 2, 3):
+        dispatch(0, k)
+    keep_own(0)
     route(1)
+    keep_own(1)
     spread(0, 0)
-    dispatch(1)
     pass_on(0, 0)
     spread(0, 1)
     spread(1, 0)

time: 45 us -> 45 us (level)
  no operation moved by 1% of the time
where the time goes in v4:
time: 45 us; the launch traced here: 44.3 us
  Pallas kernels  43.6 us (97%)
  between operations  0.64 us (1%)
    pallas_call x1, Pallas kernels, fused_body(): pl.pallas_call(kernel, out_shape=results, in_specs=[pl.BlockSpec(memory_s...  40.8 us
    pallas_call x1, Pallas kernels, fused_body(): pl.pallas_call(finish, out_shape=results, in_specs=[anywhere] * 4, out_sp...  2.81 us

profile of v4, /device:TPU:0, one launch (start us, length us, event | category | flops | bytes accessed | tf_op | source)
XLA Modules:
  0.0 44.3 jit_solution(10064588928991660151)
XLA Ops:
  0.6 40.8 %shard_map.84 = (f32[128,1024]{1,0:T(8,128)}, f32[128,1024]{1,0:T(8,128)}, f32[256,1024]{1,0:T(8,128)}, f32[1024,256]{1,0:T(8,128)}) custom-call(s32[1,32]{1,0:T(1,128)} %bitcast.9, f32[128,1024]{1,0:T(8,128)} %tokens_hbm.1, f32[128,1024]{1,0:T(8,128)} %upstream_hbm.1, bf16[1024,1024]{1,0:T(8,128)(2,1)} %bitcast.5, bf16[1024,1024]{1,0:T(8,128)(2,1)} %bitcast.6), custom_call_target="tpu_custom_call" | custom-call | flops 6442450944 | bytes 8388608 | tf_op jit(solution)/shard_map/pallas_call | solution.py:377
  41.4 2.8 %shard_map.85 = (f32[128,1024]{1,0:T(8,128)}, f32[128,1024]{1,0:T(8,128)}, f32[256,1024]{1,0:T(8,128)}, f32[1024,256]{1,0:T(8,128)}) custom-call(f32[128,1024]{1,0:T(8,128)} %get-tuple-element.12.refs_0_, f32[128,1024]{1,0:T(8,128)} %get-tuple-element.13.refs_1_, f32[256,1024]{1,0:T(8,128)} %get-tuple-element.14.refs_2_, f32[1024,256]{1,0:T(8,128)} %get-tuple-element.15.refs_3_), custom_call_target="tpu_custom_call" | custom-call | bytes 3145728 | tf_op jit(solution)/shard_map/pallas_call | solution.py:421
